TPU v7x, 512 devices: a whole 4x8x8 slice. The times are simulated.
512 devices in a mesh: dp: 32 (over y, x), context: 16 (over z, core).
Axes of the slice: x: 4, y: 8, z: 8, core: 2. Of those that a mesh axis runs over, the one named last changes fastest.
Arguments:
- queries: bfloat16 [32, 2048, 4096], P('dp', 'context'), may hold values from -152 to 152
- keys: bfloat16 [32, 2048, 512], P('dp', 'context'), may hold values from -8 to 8
- values: bfloat16 [32, 2048, 512], P('dp', 'context'), may hold values from -6 to 6
- out_grad: bfloat16 [32, 2048, 4096], P('dp', 'context'), may hold values from -6 to 6
- layer_input: bfloat16 [32, 2048, 8192], P('dp', 'context'), may hold values from -0.1875 to 0.1875
- doc_blocks: int32 [32, 5], P('dp'), may hold values from 1 to 8, 16 in all within a row
Outputs:
- key_grad: bfloat16 [32, 2048, 512], P('dp', 'context')
- wv_grad: float32 [8192, 512], P(('dp', 'context'))
Inputs may be any that keep to these rules, and one draw needn't show every extreme that they name: `doc_blocks`: each row lists, in mask blocks of 128 tokens, the lengths of the documents packed one after another into that sequence; they sum to 16, and the longest has exactly 8 blocks.
All inputs are finite; a program needn't handle non-finite values.
Results may differ from a plain program's by a relative error of at most 0.035.
Values may be sent and summed in bfloat16 or wider, within the bound.
A program may use at most 64 MiB of HBM per device.

v0:
```python
import math

import jax
import jax.numpy as jnp
from jax import lax
from jax.experimental import pallas as pl
from jax.experimental.pallas import tpu as pltpu
from jax.sharding import PartitionSpec as P

HEAD = 128
BLK = 128
NX, NY, NZ = 4, 8, 8
HOPS = 4
ROWS = 1152
MASKED = -1e30
SCALE = 1.0 / math.sqrt(HEAD)
MESH = pl.DeviceIdType.MESH
F32 = jnp.float32
BF16 = jnp.bfloat16


def place():
    d = lax.axis_index("dp")
    c = lax.axis_index("context")
    return lax.rem(d, NX), lax.div(d, NX), lax.div(c, 2), lax.rem(c, 2)


def device(x, y, z, h):
    return (y * NX + x, z * 2 + h)


def around(i, by, n):
    return lax.rem(i + (by + n), n)


class Copies:
    def __init__(self, send, recv):
        self.send, self.recv, self.used, self.all = send, recv, 0, []

    def claim(self):
        self.used += 1
        return self.used - 1

    def make(self, i, src, dst, target):
        return pltpu.make_async_remote_copy(
            src_ref=src,
            dst_ref=dst,
            send_sem=self.send.at[i],
            recv_sem=self.recv.at[i],
            device_id=target,
            device_id_type=MESH,
        )

    def remote(self, src, dst, target):
        copy = self.make(self.claim(), src, dst, target)
        copy.start()
        self.all.append(copy)
        return copy

    def local(self, src, dst):
        copy = pltpu.make_async_copy(src, dst, self.send.at[self.claim()])
        copy.start()
        return copy

    def wait_sends(self, leave=0):
        while len(self.all) > leave:
            self.all.pop(0).wait_send()


def greet(targets):
    barrier = pltpu.get_barrier_semaphore()
    for target in targets:
        pl.semaphore_signal(barrier, inc=1, device_id=target, device_id_type=MESH)
    pl.semaphore_wait(barrier, len(targets))


def lanes(start, size):
    return pl.ds(pl.multiple_of(start, 128), size)


def rows_at(start, size):
    return pl.ds(pl.multiple_of(start, 128), size)


def rows16(block):
    return pl.ds(pl.multiple_of(block * 16, 16), 16)


def fill_bias(docs, bias, z):
    ends = []
    total = docs[0, 0]
    for i in range(5):
        ends.append(total)
        if i < 4:
            total = total + docs[0, i + 1]

    def doc(b):
        return sum((b >= e).astype(jnp.int32) for e in ends)

    key = lax.broadcasted_iota(jnp.int32, (BLK, BLK), 0)
    query = lax.broadcasted_iota(jnp.int32, (BLK, BLK), 1)
    for j in range(2):
        qb = 2 * z + j
        for i in range(9):
            kb = 2 * z - 2 * (i // 2) + (1 if i == 8 else i % 2)
            if i < 2 and i == j:
                block = jnp.where(key <= query, 0.0, MASKED)
            elif i == 1 and j == 0:
                block = jnp.full((BLK, BLK), MASKED, F32)
            else:
                same = (kb >= 0) & (doc(kb) == doc(qb))
                block = jnp.full((BLK, BLK), jnp.where(same, 0.0, MASKED), F32)
            bias[pl.ds(i * BLK, BLK), pl.ds(j * BLK, BLK)] = block


def kernel(
    docs, q, g, k, v, xin, key_grad, wv_grad,
    qg, qs, kv, xs, stage, relay, bias, expo, low, top, inv, dv, dk, csend, crecv, dvt, part, ysend, yrecv, zsend, zrecv, kswap,
    send, recv,
):
    x, y, z, h = place()
    ctx = z * 2 + h
    sib = device(x, y, z, 1 - h)
    up = device(x, y, around(z, 1, NZ), h)
    down = device(x, y, around(z, -1, NZ), h)
    across = [device(around(x, dx, NX), y, z, h) for dx in range(1, NX)]
    ahead = device(x, around(y, 1, NY), z, h)
    behind = device(x, around(y, -1, NY), z, h)
    column = [(y * NX + x, around(ctx, o, 16)) for o in range(1, 16)]
    mine = rows_at(h * BLK, BLK)
    copies = Copies(send, recv)

    def x_rows(dx):
        return rows_at(dx * 256 + h * BLK, BLK)

    own_k, own_v = [
        [
            copies.local(src.at[:, lanes((2 * h + a) * HEAD, HEAD)], kv.at[a, j, mine])
            for a in range(2)
        ]
        for j, src in enumerate((k, v))
    ]
    own_q = [
        copies.local(src.at[:, lanes(h * 2048, 2048)], qg.at[j, mine])
        for j, src in enumerate((q, g))
    ]
    stage_sem = send.at[copies.claim()]
    for dx in (2, 1, 3, 0):
        to = around(x, dx, NX)
        for c in range(NY):
            src = xin.at[:, lanes(c * 1024 + to * 256, 256)]
            dst = xs.at[c, x_rows(0)] if dx == 0 else stage.at[dx, c]
            pltpu.make_async_copy(src, dst, stage_sem).start()

    def staged():
        pltpu.make_async_copy(stage, stage, stage_sem).wait()

    greet(column + across + [ahead, behind])

    up_other = device(x, y, around(z, 1, NZ), 1 - h)
    hops, swapped = {}, {}

    def first_hop(j, src):
        for a in range(2):
            own = src.at[:, lanes((2 * h + a) * HEAD, HEAD)]
            other = src.at[:, lanes((2 * (1 - h) + a) * HEAD, HEAD)]
            dst = kv.at[a, j, rows_at(256 + h * BLK, BLK)]
            hops[j, a] = [copies.remote(own, dst, up), copies.remote(other, dst, up_other)]

    def swap_kv(j, src):
        for a in range(2):
            other = src.at[:, lanes((2 * (1 - h) + a) * HEAD, HEAD)]
            swapped[j, a] = copies.remote(other, kv.at[a, j, mine], sib)

    def arrived(j, a):
        for copy in hops[j, a]:
            copy.wait_recv()

    def hop(j, a, step):
        arrived(j, a)
        lo, size = (768 + 128, 128) if step == 4 else ((step - 1) * 256, 256)
        hops[j, a] = [
            copies.remote(kv.at[a, j, pl.ds(lo, size)], kv.at[a, j, pl.ds(step * 256, size)], up)
        ]

    first_hop(0, k)
    swap_kv(0, k)
    exchange = [
        copies.remote(src.at[:, lanes((1 - h) * 2048, 2048)], qg.at[j, mine], sib)
        for j, src in enumerate((q, g))
    ]

    own_x, spread_x, relays, second, pieces = [], [], [], [], []
    ways = []
    for way in (h, 1 - h):
        dx = 1 + 2 * way
        ways.append((way, dx, device(around(x, dx, NX), y, z, h)))

    def x_part(dx, lo=0, size=NY):
        return xs.at[pl.ds(lo, size), x_rows(dx)]

    for way, dx, target in ways:
        far = pl.ds(way * 4, 4)
        pieces.append((stage.at[2, far], relay.at[way], target, relays))
    for lo in (0, 4):
        for way, dx, target in ways:
            pieces.append((stage.at[dx, pl.ds(lo, 4)], x_part(dx, lo, 4), target, spread_x))

    def feed(n):
        for _ in range(n):
            src, dst, target, group = pieces.pop(0)
            group.append(copies.remote(src, dst, target))

    def relay_on():
        for i, (way, dx, target) in enumerate(ways):
            relays[i].wait_recv()
            second.append(copies.remote(relay.at[way], x_part(2, way * 4, 4), target))

    passed = {}

    def pass_on(dx):
        passed[len(passed)] = copies.remote(x_part(dx), x_part(dx), sib)

    def pass_own():
        pass_on(0)

    def pass_near():
        for copy in spread_x:
            copy.wait_recv()
        for way, dx, target in ways:
            pass_on(dx)

    def pass_far():
        for copy in second:
            copy.wait_recv()
        pass_on(2)

    contract = (((1,), (1,)), ((), ()))

    def slot_rows(slot):
        return pl.ds(slot * 256, 128 if slot == 4 else 256)

    def heads(one, *args):
        @pl.loop(0, 4)
        def _(i):
            one(*args, 2 * i)
            one(*args, 2 * i + 1)

    def score(a, slot, head):
        rows = slot_rows(slot)
        col = lanes((a * 8 + head) * HEAD, HEAD)
        s = lax.dot_general(kv[a, 0, rows], qg[0, :, col], contract, preferred_element_type=F32)
        t = s * (SCALE * math.log2(math.e)) + bias[rows, :]
        expo[a, rows, lanes(head * 256, 256)] = t
        highest = jnp.max(t.reshape(-1, 8, 256), axis=0)
        if slot > 0:
            highest = jnp.maximum(highest, top[a * 8 + head])
        top[a * 8 + head] = highest

    def weigh(a, head):
        cols = lanes(head * 256, 256)
        m = jnp.max(top[a * 8 + head], axis=0, keepdims=True)
        e = jnp.exp2(expo[a, :, cols] - m)
        expo[a, :, cols] = e
        r = 1.0 / jnp.sum(e, axis=0, keepdims=True)
        inv[a * 8 + head] = r
        low[a, :, cols] = (e * r).astype(BF16)

    def push_back(a, head):
        cols = lanes(head * 256, 256)
        col = lanes((a * 8 + head) * HEAD, HEAD)
        dp = lax.dot_general(kv[a, 1], qg[1, :, col], contract, preferred_element_type=F32)
        p = expo[a, :, cols] * inv[a * 8 + head]
        delta = jnp.sum(p * dp, axis=0, keepdims=True)
        low[a, :, cols] = (p * (dp - delta)).astype(BF16)

    def sum_heads(w, a, slot):
        rows = slot_rows(slot)
        parts[w][a, rows] = jnp.dot(low[a, rows], qs[1 - w, a], preferred_element_type=F32)

    parts = (dv, dk)
    chain = {}

    def chain_step(w, a, step):
        i = 2 * w + a
        if step > 1:
            chain[i].wait_recv()
        if step == 1:
            csend[i, 0, pl.ds(0, 128)] = parts[w][a, pl.ds(1024, 128)].astype(BF16)
            src, dst = csend.at[i, 0, pl.ds(0, 128)], crecv.at[i, 0, pl.ds(0, 128)]
        else:
            here = parts[w][a, pl.ds((5 - step) * 256, 256)]
            if step == 2:
                csend[i, 1, pl.ds(0, 128)] = here[:128].astype(BF16)
                csend[i, 1, pl.ds(128, 128)] = (
                    here[128:] + crecv[i, 0, pl.ds(0, 128)].astype(F32)
                ).astype(BF16)
            else:
                csend[i, step - 1] = (here + crecv[i, step - 2].astype(F32)).astype(BF16)
            src, dst = csend.at[i, step - 1], crecv.at[i, step - 1]
        chain[i] = copies.remote(src, dst, down)

    def chain_end(w, a):
        i = 2 * w + a
        chain[i].wait_recv()
        return parts[w][a, pl.ds(0, 256)] + crecv[i, 3].astype(F32)

    spread = {}

    def spread_dv(a):
        dvt[a, :, 0:256] = chain_end(0, a).T.astype(BF16)
        for dx in (2, 1, 3):
            spread[a, dx] = copies.remote(
                dvt.at[a, :, pl.ds(0, 256)], dvt.at[a, :, pl.ds(dx * 256, 256)], across[dx - 1]
            )

    def wait_x():
        for n in range(NX):
            passed[n].wait_recv()

    def product(a):
        for dx in range(1, NX):
            spread[a, dx].wait_recv()

        def chunk(c):
            part[a, c] = jnp.dot(dvt[a], xs[c], preferred_element_type=F32)

        near = 3 + 2 * (1 - h)
        chunk(around(y, 4, NY))
        chunk(around(y, near, NY))
        ring_step(a, 1)

        @pl.loop(0, 6)
        def _(i):
            chunk(lax.rem(y + near + 1 + h + i, NY))

    lengths = {(0, 0): 4, (0, 1): 3, (1, 0): 4, (1, 1): 3}
    ring, direct = {}, {}
    sides = []
    for way in (h, 1 - h):
        sign = 1 - 2 * way
        sides.append((sign, device(x, around(y, sign, NY), z, h)))

    def ring_step(a, step):
        for s, (sign, target) in enumerate(sides):
            n = lengths[a, s]
            if step > n:
                continue
            here = part[a, around(y, sign * (n - step + 1), NY)]
            if step > 1:
                ring[a, s].wait_recv()
                here = here + yrecv[a, s, step - 2].astype(F32)
            ysend[a, s, step - 1] = here.astype(BF16)
            ring[a, s] = copies.remote(
                ysend.at[a, s, step - 1], yrecv.at[a, s, step - 1], target
            )

    def ring_end(a):
        for s in range(2):
            ring[a, s].wait_recv()
        total = (
            part[a, y]
            + yrecv[a, 0, lengths[a, 0] - 1].astype(F32)
            + yrecv[a, 1, lengths[a, 1] - 1].astype(F32)
        )
        zsend[a] = total.T.astype(BF16)
        direct[a] = [
            copies.remote(zsend.at[a, rows16(around(ctx, o, 16))], zrecv.at[a, o], column[o - 1])
            for o in range(1, 16)
        ]

    fill_bias(docs, bias, z)
    staged()
    feed(2)
    for copy in own_q:
        copy.wait()
    exchange[0].wait_recv()
    for slot in range(4):
        for a in range(2):
            if slot < 3:
                hop(0, a, slot + 2)
            if slot == 0:
                swapped[0, a].wait_recv()
                own_k[a].wait()
            heads(score, a, slot)
        if slot == 0:
            swap_kv(1, v)
            feed(2)
        if slot == 1:
            first_hop(1, v)
        if slot == 2:
            feed(2)
    for a in range(2):
        hop(1, a, 2)
    relay_on()
    exchange[1].wait_recv()

    @pl.loop(0, 16)
    def _(i):
        a, head = lax.div(i, 8), lax.rem(i, 8)
        for j in range(2):
            qs[j, a, rows_at(head * 256, 256)] = qg[j, :, lanes(i * HEAD, HEAD)]

    arrived(0, 0)
    heads(score, 0, 4)
    heads(weigh, 0)
    sum_heads(0, 0, 4)
    chain_step(0, 0, 1)
    arrived(0, 1)
    heads(score, 1, 4)
    for a in range(2):
        hop(1, a, 3)
    heads(weigh, 1)
    sum_heads(0, 1, 4)
    chain_step(0, 1, 1)
    for a in range(2):
        hop(1, a, 4)
    sum_heads(0, 0, 3)
    chain_step(0, 0, 2)
    sum_heads(0, 1, 3)
    pass_own()
    for slot in (2, 1, 0):
        sum_heads(0, 0, slot)
    chain_step(0, 1, 2)
    for slot in (2, 1, 0):
        sum_heads(0, 1, slot)
    chain_step(0, 0, 3)

    for a in range(2):
        arrived(1, a)
        swapped[1, a].wait_recv()
        own_v[a].wait()
    order = [(a, head) for a in range(2) for head in range(8)]

    def some(n):
        for _ in range(n):
            push_back(*order.pop(0))

    some(2)
    chain_step(0, 1, 3)
    some(1)
    chain_step(0, 0, 4)
    some(3)
    chain_step(0, 1, 4)
    some(1)
    spread_dv(0)
    pass_near()
    some(1)
    sum_heads(1, 0, 4)
    chain_step(1, 0, 1)
    for slot in (3, 2, 1, 0):
        sum_heads(1, 0, slot)
    spread_dv(1)
    some(2)
    pass_far()
    chain_step(1, 0, 2)
    some(2)
    copies.wait_sends(8)
    wait_x()
    product(0)
    chain_step(1, 0, 3)
    some(2)
    ring_step(0, 2)
    product(1)
    some(2)
    ring_step(0, 3)
    ring_step(1, 2)
    sum_heads(1, 1, 4)
    chain_step(1, 1, 1)
    chain_step(1, 0, 4)
    for slot in (3, 2, 1, 0):
        sum_heads(1, 1, slot)
    ring_step(0, 4)
    ring_step(1, 3)
    chain_step(1, 1, 2)
    copies.wait_sends(8)
    ring_step(1, 4)
    ring_end(0)
    chain_step(1, 1, 3)
    ring_end(1)
    chain_step(1, 1, 4)
    copies.wait_sends(32)
    kswap[0, :, 0:HEAD] = (chain_end(1, 0) * SCALE).astype(BF16)
    kswap[0, :, HEAD : 2 * HEAD] = (chain_end(1, 1) * SCALE).astype(BF16)
    swap = copies.remote(
        kswap.at[0, rows_at((1 - h) * BLK, BLK)], kswap.at[1, pl.ds(0, BLK)], sib
    )
    key_grad[:, lanes(h * 256, 256)] = kswap[0, rows_at(h * BLK, BLK), :]
    for a in range(2):
        sums = [zsend[a, rows16(ctx), :].astype(F32), None]
        for o in range(1, 16):
            direct[a][o - 1].wait_recv()
            got = zrecv[a, o].astype(F32)
            sums[o % 2] = got if sums[o % 2] is None else sums[o % 2] + got
        wv_grad[:, lanes(h * 256 + a * HEAD, HEAD)] = sums[0]
        wv_grad[:, lanes((1 - h) * 256 + a * HEAD, HEAD)] = sums[1]
    swap.wait_recv()
    key_grad[:, lanes((1 - h) * 256, 256)] = kswap[1, pl.ds(0, BLK), :]
    copies.wait_sends()


def on_device(queries, keys, values, out_grad, layer_input, doc_blocks):
    anywhere = pl.BlockSpec(memory_space=pl.ANY)
    in_vmem = pl.BlockSpec(memory_space=pltpu.VMEM)
    key_grad, wv_grad = pl.pallas_call(
        kernel,
        out_shape=(
            jax.ShapeDtypeStruct((BLK, 512), BF16),
            jax.ShapeDtypeStruct((16, 512), F32),
        ),
        in_specs=[pl.BlockSpec(memory_space=pltpu.SMEM)] + [anywhere] * 5,
        out_specs=(in_vmem, in_vmem),
        scratch_shapes=[
            pltpu.VMEM((2, 256, 2048), BF16),
            pltpu.VMEM((2, 2, 2048, HEAD), BF16),
            pltpu.VMEM((2, 2, ROWS, HEAD), BF16),
            pltpu.VMEM((NY, NX * 256, 256), BF16),
            pltpu.VMEM((NX, NY, BLK, 256), BF16),
            pltpu.VMEM((2, 4, BLK, 256), BF16),
            pltpu.VMEM((ROWS, 256), F32),
            pltpu.VMEM((2, ROWS, 2048), F32),
            pltpu.VMEM((2, ROWS, 2048), BF16),
            pltpu.VMEM((16, 8, 256), F32),
            pltpu.VMEM((16, 1, 256), F32),
            pltpu.VMEM((2, ROWS, HEAD), F32),
            pltpu.VMEM((2, ROWS, HEAD), F32),
            pltpu.VMEM((4, HOPS, 256, HEAD), BF16),
            pltpu.VMEM((4, HOPS, 256, HEAD), BF16),
            pltpu.VMEM((2, HEAD, NX * 256), BF16),
            pltpu.VMEM((2, NY, HEAD, 256), F32),
            pltpu.VMEM((2, 2, 4, HEAD, 256), BF16),
            pltpu.VMEM((2, 2, 4, HEAD, 256), BF16),
            pltpu.VMEM((2, 256, HEAD), BF16),
            pltpu.VMEM((2, 16, 16, HEAD), BF16),
            pltpu.VMEM((2, 256, 256), BF16),
            pltpu.SemaphoreType.DMA((144,)),
            pltpu.SemaphoreType.DMA((144,)),
        ],
        compiler_params=pltpu.CompilerParams(
            collective_id=0, has_side_effects=True, vmem_limit_bytes=56 << 20
        ),
        name="grads",
    )(doc_blocks, queries[0], out_grad[0], keys[0], values[0], layer_input[0])
    return (key_grad[None], wv_grad)


def solution(mesh):
    in_specs = (
        P("dp", "context", None),
        P("dp", "context", None),
        P("dp", "context", None),
        P("dp", "context", None),
        P("dp", "context", None),
        P("dp", None),
    )
    out_specs = (P("dp", "context", None), P(("dp", "context"), None))
    return jax.shard_map(
        on_device, mesh=mesh, in_specs=in_specs, out_specs=out_specs, check_vma=False
    )
```

profile of v0, /device:TPU:1, one launch (start us, length us, event | category | flops | bytes accessed | tf_op | source)
XLA Modules:
  0.0 91.0 jit_solution(17240866691126155685)
XLA Ops:
  0.6 87.4 %grads.1 = (bf16[128,512]{1,0:T(8,128)(2,1)}, f32[16,512]{1,0:T(8,128)}) custom-call(s32[1,5]{1,0:T(1,128)} %docs.1, bf16[128,4096]{1,0:T(8,128)(2,1)} %bitcast.7, bf16[128,4096]{1,0:T(8,128)(2,1)} %bitcast.8, bf16[128,512]{1,0:T(8,128)(2,1)} %bitcast.9, bf16[128,512]{1,0:T(8,128)(2,1)} %bitcast.10, bf16[128,8192]{1,0:T(8,128)(2,1)} %bitcast.6), custom_call_target="tpu_custom_call" | custom-call | tf_op jit(solution)/shard_map/grads/pallas_call | solution.py:505
  88.0 1.6 %copy.10 = bf16[1,128,512]{2,1,0:T(8,128)(2,1)} copy(bf16[1,128,512]{2,1,0:T(8,128)(2,1)} %bitcast.11) | data formatting | bytes 262144
  89.6 1.4 %copy.11 = f32[16,512]{1,0:T(8,128)} copy(f32[16,512]{1,0:T(8,128)} %get-tuple-element.9) | data formatting | bytes 65536
where the time goes:
time: 91.2 us; the launch traced here: 91 us
  Pallas kernels  87.4 us (96%)
  local copies, waits for them, and re-layouts  2.94 us (3%)
    pallas_call x1, Pallas kernels, on_device(): pl.pallas_call(kernel, out_shape=(jax.ShapeDtypeStruct((BLK, 512), BF16),...  87.4 us
    unnamed x2, local copies, waits for them, and re-layouts  2.94 us

commit v1 on v0

--- a/solution.py
+++ b/solution.py
@@ -115,7 +115,7 @@
 
 def kernel(
     docs, q, g, k, v, xin, key_grad, wv_grad,
-    qg, qs, kv, xs, stage, relay, bias, expo, low, top, inv, dv, dk, csend, crecv, dvt, part, ysend, yrecv, zsend, zrecv, kswap,
+    qg, qs, kv, xs, stage, relay, bias, expo, low, top, inv, dv, dk, csend, crecv, dvt, ysend, yrecv, zsend, zrecv, kswap,
     send, recv,
 ):
     x, y, z, h = place()
@@ -144,16 +144,20 @@
         copies.local(src.at[:, lanes(h * 2048, 2048)], qg.at[j, mine])
         for j, src in enumerate((q, g))
     ]
-    stage_sem = send.at[copies.claim()]
+    stage_sem, own_x_sem = send.at[copies.claim()], send.at[copies.claim()]
     for dx in (2, 1, 3, 0):
         to = around(x, dx, NX)
         for c in range(NY):
             src = xin.at[:, lanes(c * 1024 + to * 256, 256)]
-            dst = xs.at[c, x_rows(0)] if dx == 0 else stage.at[dx, c]
-            pltpu.make_async_copy(src, dst, stage_sem).start()
+            if dx == 0:
+                pltpu.make_async_copy(src, xs.at[c, x_rows(0)], own_x_sem).start()
+            else:
+                pltpu.make_async_copy(src, stage.at[dx - 1, c], stage_sem).start()
 
     def staged():
         pltpu.make_async_copy(stage, stage, stage_sem).wait()
+        own = xs.at[:, x_rows(0)]
+        pltpu.make_async_copy(own, own, own_x_sem).wait()
 
     greet(column + across + [ahead, behind])
 
@@ -201,10 +205,10 @@
 
     for way, dx, target in ways:
         far = pl.ds(way * 4, 4)
-        pieces.append((stage.at[2, far], relay.at[way], target, relays))
+        pieces.append((stage.at[1, far], relay.at[way], target, relays))
     for lo in (0, 4):
         for way, dx, target in ways:
-            pieces.append((stage.at[dx, pl.ds(lo, 4)], x_part(dx, lo, 4), target, spread_x))
+            pieces.append((stage.at[dx - 1, pl.ds(lo, 4)], x_part(dx, lo, 4), target, spread_x))
 
     def feed(n):
         for _ in range(n):
@@ -241,10 +245,10 @@
         return pl.ds(slot * 256, 128 if slot == 4 else 256)
 
     def heads(one, *args):
-        @pl.loop(0, 4)
+        @pl.loop(0, 2)
         def _(i):
-            one(*args, 2 * i)
-            one(*args, 2 * i + 1)
+            for j in range(4):
+                one(*args, 4 * i + j)
 
     def score(a, slot, head):
         rows = slot_rows(slot)
@@ -318,12 +322,19 @@
         for n in range(NX):
             passed[n].wait_recv()
 
+    part = expo.at[0]
+
+    def partial(a, c):
+        return part[rows_at(c * HEAD, HEAD), a * 256 : (a + 1) * 256]
+
     def product(a):
         for dx in range(1, NX):
             spread[a, dx].wait_recv()
 
         def chunk(c):
-            part[a, c] = jnp.dot(dvt[a], xs[c], preferred_element_type=F32)
+            part[rows_at(c * HEAD, HEAD), a * 256 : (a + 1) * 256] = jnp.dot(
+                dvt[a], xs[c], preferred_element_type=F32
+            )
 
         near = 3 + 2 * (1 - h)
         chunk(around(y, 4, NY))
@@ -346,7 +357,7 @@
             n = lengths[a, s]
             if step > n:
                 continue
-            here = part[a, around(y, sign * (n - step + 1), NY)]
+            here = partial(a, around(y, sign * (n - step + 1), NY))
             if step > 1:
                 ring[a, s].wait_recv()
                 here = here + yrecv[a, s, step - 2].astype(F32)
@@ -359,7 +370,7 @@
         for s in range(2):
             ring[a, s].wait_recv()
         total = (
-            part[a, y]
+            partial(a, y)
             + yrecv[a, 0, lengths[a, 0] - 1].astype(F32)
             + yrecv[a, 1, lengths[a, 1] - 1].astype(F32)
         )
@@ -410,21 +421,25 @@
     heads(score, 1, 4)
     for a in range(2):
         hop(1, a, 3)
-    heads(weigh, 1)
+    for head in range(8):
+        weigh(1, head)
+        if head == 1:
+            sum_heads(0, 0, 3)
+        elif head == 4:
+            chain_step(0, 0, 2)
+            sum_heads(0, 0, 2)
+        elif head == 6:
+            sum_heads(0, 0, 1)
     sum_heads(0, 1, 4)
     chain_step(0, 1, 1)
     for a in range(2):
         hop(1, a, 4)
-    sum_heads(0, 0, 3)
-    chain_step(0, 0, 2)
     sum_heads(0, 1, 3)
+    sum_heads(0, 0, 0)
+    sum_heads(0, 1, 2)
     pass_own()
-    for slot in (2, 1, 0):
-        sum_heads(0, 0, slot)
+    chain_step(0, 0, 3)
     chain_step(0, 1, 2)
-    for slot in (2, 1, 0):
-        sum_heads(0, 1, slot)
-    chain_step(0, 0, 3)
 
     for a in range(2):
         arrived(1, a)
@@ -436,6 +451,8 @@
         for _ in range(n):
             push_back(*order.pop(0))
 
+    sum_heads(0, 1, 1)
+    sum_heads(0, 1, 0)
     some(2)
     chain_step(0, 1, 3)
     some(1)
@@ -448,10 +465,13 @@
     some(1)
     sum_heads(1, 0, 4)
     chain_step(1, 0, 1)
-    for slot in (3, 2, 1, 0):
-        sum_heads(1, 0, slot)
+    sum_heads(1, 0, 3)
+    some(1)
     spread_dv(1)
-    some(2)
+    sum_heads(1, 0, 2)
+    sum_heads(1, 0, 1)
+    sum_heads(1, 0, 0)
+    some(1)
     pass_far()
     chain_step(1, 0, 2)
     some(2)
@@ -515,7 +535,7 @@
             pltpu.VMEM((2, 2, 2048, HEAD), BF16),
             pltpu.VMEM((2, 2, ROWS, HEAD), BF16),
             pltpu.VMEM((NY, NX * 256, 256), BF16),
-            pltpu.VMEM((NX, NY, BLK, 256), BF16),
+            pltpu.VMEM((NX - 1, NY, BLK, 256), BF16),
             pltpu.VMEM((2, 4, BLK, 256), BF16),
             pltpu.VMEM((ROWS, 256), F32),
             pltpu.VMEM((2, ROWS, 2048), F32),
@@ -527,7 +547,6 @@
             pltpu.VMEM((4, HOPS, 256, HEAD), BF16),
             pltpu.VMEM((4, HOPS, 256, HEAD), BF16),
             pltpu.VMEM((2, HEAD, NX * 256), BF16),
-            pltpu.VMEM((2, NY, HEAD, 256), F32),
             pltpu.VMEM((2, 2, 4, HEAD, 256), BF16),
             pltpu.VMEM((2, 2, 4, HEAD, 256), BF16),
             pltpu.VMEM((2, 256, HEAD), BF16),
@@ -537,7 +556,7 @@
             pltpu.SemaphoreType.DMA((144,)),
         ],
         compiler_params=pltpu.CompilerParams(
-            collective_id=0, has_side_effects=True, vmem_limit_bytes=56 << 20
+            collective_id=0, has_side_effects=True, vmem_limit_bytes=56307712
         ),
         name="grads",
     )(doc_blocks, queries[0], out_grad[0], keys[0], values[0], layer_input[0])

time: 91.2 us -> 89.6 us (0.982)
  local copies, waits for them, and re-layouts: 2.94 us -> 1.92 us
    unnamed x2 -> x4, local copies, waits for them, and re-layouts: 2.94 us -> 1.92 us
where the time goes in v1:
time: 89.6 us; the launch traced here: 89.5 us
  Pallas kernels  86.9 us (97%)
  local copies, waits for them, and re-layouts  1.92 us (2%)
    pallas_call x1, Pallas kernels, on_device(): pl.pallas_call(kernel, out_shape=(jax.ShapeDtypeStruct((BLK, 512), BF16),...  86.9 us
    unnamed x4, local copies, waits for them, and re-layouts  1.92 us

profile of v1, /device:TPU:1, one launch (start us, length us, event | category | flops | bytes accessed | tf_op | source)
XLA Modules:
  0.0 89.5 jit_solution(1651641013979821619)
XLA Ops:
  0.6 0.0 copy-start
  0.6 0.6 copy-done
  1.3 86.9 %grads.1 = (bf16[128,512]{1,0:T(8,128)(2,1)S(1)}, f32[16,512]{1,0:T(8,128)S(1)}) custom-call(s32[1,5]{1,0:T(1,128)S(1)} %copy-done, bf16[128,4096]{1,0:T(8,128)(2,1)} %bitcast.8, bf16[128,4096]{1,0:T(8,128)(2,1)} %bitcast.9, bf16[128,512]{1,0:T(8,128)(2,1)} %bitcast.10, bf16[128,512]{1,0:T(8,128)(2,1)} %bitcast.11, bf16[128,8192]{1,0:T(8,128)(2,1)} %bitcast.7), custom_call_target="tpu_custom_call" | custom-call | tf_op jit(solution)/shard_map/grads/pallas_call | solution.py:525
  88.2 0.7 copy.10
  88.9 0.6 copy.11
Async XLA Ops:
  0.6 0.7 copy-start

commit v2 on v1

--- a/solution.py
+++ b/solution.py
@@ -461,7 +461,6 @@
     chain_step(0, 1, 4)
     some(1)
     spread_dv(0)
-    pass_near()
     some(1)
     sum_heads(1, 0, 4)
     chain_step(1, 0, 1)
@@ -472,33 +471,35 @@
     sum_heads(1, 0, 1)
     sum_heads(1, 0, 0)
     some(1)
+    chain_step(1, 0, 2)
+    some(3)
+    chain_step(1, 0, 3)
+    some(3)
+    sum_heads(1, 1, 4)
+    chain_step(1, 1, 1)
+    sum_heads(1, 1, 3)
+    chain_step(1, 0, 4)
+    pass_near()
+    sum_heads(1, 1, 2)
+    sum_heads(1, 1, 1)
+    sum_heads(1, 1, 0)
+    chain_step(1, 1, 2)
     pass_far()
-    chain_step(1, 0, 2)
-    some(2)
     copies.wait_sends(8)
     wait_x()
     product(0)
-    chain_step(1, 0, 3)
-    some(2)
+    product(1)
+    chain_step(1, 1, 3)
     ring_step(0, 2)
-    product(1)
-    some(2)
+    ring_step(1, 2)
+    chain_step(1, 1, 4)
     ring_step(0, 3)
-    ring_step(1, 2)
-    sum_heads(1, 1, 4)
-    chain_step(1, 1, 1)
-    chain_step(1, 0, 4)
-    for slot in (3, 2, 1, 0):
-        sum_heads(1, 1, slot)
+    ring_step(1, 3)
+    copies.wait_sends(8)
     ring_step(0, 4)
-    ring_step(1, 3)
-    chain_step(1, 1, 2)
-    copies.wait_sends(8)
     ring_step(1, 4)
     ring_end(0)
-    chain_step(1, 1, 3)
     ring_end(1)
-    chain_step(1, 1, 4)
     copies.wait_sends(32)
     kswap[0, :, 0:HEAD] = (chain_end(1, 0) * SCALE).astype(BF16)
     kswap[0, :, HEAD : 2 * HEAD] = (chain_end(1, 1) * SCALE).astype(BF16)

time: 89.6 us -> 91.9 us (1.026)
  Pallas kernels: 86.9 us -> 89.2 us
    pallas_call x1, Pallas kernels: 86.9 us -> 89.2 us  [on_device(): pl.pallas_call(kernel, out_shape=(jax.ShapeDtypeStruct((BLK, 512), BF16),...]
where the time goes in v2:
time: 91.9 us; the launch traced here: 91.8 us
  Pallas kernels  89.2 us (97%)
  local copies, waits for them, and re-layouts  1.92 us (2%)
    pallas_call x1, Pallas kernels, on_device(): pl.pallas_call(kernel, out_shape=(jax.ShapeDtypeStruct((BLK, 512), BF16),...  89.2 us
    unnamed x4, local copies, waits for them, and re-layouts  1.92 us

profile of v2, /device:TPU:1, one launch (start us, length us, event | category | flops | bytes accessed | tf_op | source)
XLA Modules:
  0.0 91.8 jit_solution(12102062123487438253)
XLA Ops:
  0.6 0.0 copy-start
  0.6 0.6 copy-done
  1.3 89.2 %grads.1 = (bf16[128,512]{1,0:T(8,128)(2,1)S(1)}, f32[16,512]{1,0:T(8,128)S(1)}) custom-call(s32[1,5]{1,0:T(1,128)S(1)} %copy-done, bf16[128,4096]{1,0:T(8,128)(2,1)} %bitcast.8, bf16[128,4096]{1,0:T(8,128)(2,1)} %bitcast.9, bf16[128,512]{1,0:T(8,128)(2,1)} %bitcast.10, bf16[128,512]{1,0:T(8,128)(2,1)} %bitcast.11, bf16[128,8192]{1,0:T(8,128)(2,1)} %bitcast.7), custom_call_target="tpu_custom_call" | custom-call | tf_op jit(solution)/shard_map/grads/pallas_call | solution.py:526
  90.5 0.7 copy.10
  91.2 0.6 copy.11
Async XLA Ops:
  0.6 0.7 copy-start

commit v3 on v1

--- a/solution.py
+++ b/solution.py
@@ -71,7 +71,10 @@
     barrier = pltpu.get_barrier_semaphore()
     for target in targets:
         pl.semaphore_signal(barrier, inc=1, device_id=target, device_id_type=MESH)
-    pl.semaphore_wait(barrier, len(targets))
+
+
+def greeted(count):
+    pl.semaphore_wait(pltpu.get_barrier_semaphore(), count)
 
 
 def lanes(start, size):
@@ -129,6 +132,8 @@
     column = [(y * NX + x, around(ctx, o, 16)) for o in range(1, 16)]
     mine = rows_at(h * BLK, BLK)
     copies = Copies(send, recv)
+    partners = column + across + [ahead, behind]
+    greet(partners)
 
     def x_rows(dx):
         return rows_at(dx * 256 + h * BLK, BLK)
@@ -159,7 +164,7 @@
         own = xs.at[:, x_rows(0)]
         pltpu.make_async_copy(own, own, own_x_sem).wait()
 
-    greet(column + across + [ahead, behind])
+    greeted(len(partners))
 
     up_other = device(x, y, around(z, 1, NZ), 1 - h)
     hops, swapped = {}, {}
@@ -263,20 +268,24 @@
 
     def weigh(a, head):
         cols = lanes(head * 256, 256)
+        col = lanes((a * 8 + head) * HEAD, HEAD)
         m = jnp.max(top[a * 8 + head], axis=0, keepdims=True)
         e = jnp.exp2(expo[a, :, cols] - m)
         expo[a, :, cols] = e
+        low[a, :, cols] = e.astype(BF16)
         r = 1.0 / jnp.sum(e, axis=0, keepdims=True)
         inv[a * 8 + head] = r
-        low[a, :, cols] = (e * r).astype(BF16)
+        by_row = jnp.broadcast_to(r, (HEAD, 256)).T
+        for j in range(2):
+            qs[j, a, rows_at(head * 256, 256)] = (qg[j, :, col].astype(F32) * by_row).astype(BF16)
 
     def push_back(a, head):
         cols = lanes(head * 256, 256)
         col = lanes((a * 8 + head) * HEAD, HEAD)
         dp = lax.dot_general(kv[a, 1], qg[1, :, col], contract, preferred_element_type=F32)
-        p = expo[a, :, cols] * inv[a * 8 + head]
-        delta = jnp.sum(p * dp, axis=0, keepdims=True)
-        low[a, :, cols] = (p * (dp - delta)).astype(BF16)
+        e = expo[a, :, cols]
+        delta = jnp.sum(e * dp, axis=0, keepdims=True) * inv[a * 8 + head]
+        low[a, :, cols] = (e * (dp - delta)).astype(BF16)
 
     def sum_heads(w, a, slot):
         rows = slot_rows(slot)
@@ -405,12 +414,6 @@
         hop(1, a, 2)
     relay_on()
     exchange[1].wait_recv()
-
-    @pl.loop(0, 16)
-    def _(i):
-        a, head = lax.div(i, 8), lax.rem(i, 8)
-        for j in range(2):
-            qs[j, a, rows_at(head * 256, 256)] = qg[j, :, lanes(i * HEAD, HEAD)]
 
     arrived(0, 0)
     heads(score, 0, 4)

time: 89.6 us -> 89.6 us (level)
  no operation moved by 1% of the time
where the time goes in v3:
time: 89.6 us; the launch traced here: 89.5 us
  Pallas kernels  86.9 us (97%)
  local copies, waits for them, and re-layouts  1.92 us (2%)
    pallas_call x1, Pallas kernels, on_device(): pl.pallas_call(kernel, out_shape=(jax.ShapeDtypeStruct((BLK, 512), BF16),...  86.9 us
    unnamed x4, local copies, waits for them, and re-layouts  1.92 us

profile of v3, /device:TPU:1, one launch (start us, length us, event | category | flops | bytes accessed | tf_op | source)
XLA Modules:
  0.0 89.5 jit_solution(8725565153919201918)
XLA Ops:
  0.6 0.0 copy-start
  0.6 0.6 copy-done
  1.3 86.9 %grads.1 = (bf16[128,512]{1,0:T(8,128)(2,1)S(1)}, f32[16,512]{1,0:T(8,128)S(1)}) custom-call(s32[1,5]{1,0:T(1,128)S(1)} %copy-done, bf16[128,4096]{1,0:T(8,128)(2,1)} %bitcast.8, bf16[128,4096]{1,0:T(8,128)(2,1)} %bitcast.9, bf16[128,512]{1,0:T(8,128)(2,1)} %bitcast.10, bf16[128,512]{1,0:T(8,128)(2,1)} %bitcast.11, bf16[128,8192]{1,0:T(8,128)(2,1)} %bitcast.7), custom_call_target="tpu_custom_call" | custom-call | tf_op jit(solution)/shard_map/grads/pallas_call | solution.py:528
  88.2 0.7 copy.10
  88.9 0.6 copy.11
Async XLA Ops:
  0.6 0.7 copy-start

commit v4 on v3

--- a/solution.py
+++ b/solution.py
@@ -254,6 +254,10 @@
         def _(i):
             for j in range(4):
                 one(*args, 4 * i + j)
+
+    def hops_of_values(step):
+        for a in range(2):
+            hop(1, a, step)
 
     def score(a, slot, head):
         rows = slot_rows(slot)
@@ -417,13 +421,14 @@
 
     arrived(0, 0)
     heads(score, 0, 4)
-    heads(weigh, 0)
+    for head in range(8):
+        weigh(0, head)
+        if head == 4:
+            hops_of_values(3)
     sum_heads(0, 0, 4)
     chain_step(0, 0, 1)
     arrived(0, 1)
     heads(score, 1, 4)
-    for a in range(2):
-        hop(1, a, 3)
     for head in range(8):
         weigh(1, head)
         if head == 1:
@@ -431,12 +436,12 @@
         elif head == 4:
             chain_step(0, 0, 2)
             sum_heads(0, 0, 2)
+        elif head == 5:
+            hops_of_values(4)
         elif head == 6:
             sum_heads(0, 0, 1)
     sum_heads(0, 1, 4)
     chain_step(0, 1, 1)
-    for a in range(2):
-        hop(1, a, 4)
     sum_heads(0, 1, 3)
     sum_heads(0, 0, 0)
     sum_heads(0, 1, 2)
@@ -444,10 +449,12 @@
     chain_step(0, 0, 3)
     chain_step(0, 1, 2)
 
-    for a in range(2):
+    def values_here(a):
         arrived(1, a)
         swapped[1, a].wait_recv()
         own_v[a].wait()
+
+    values_here(0)
     order = [(a, head) for a in range(2) for head in range(8)]
 
     def some(n):
@@ -469,6 +476,7 @@
     sum_heads(1, 0, 4)
     chain_step(1, 0, 1)
     sum_heads(1, 0, 3)
+    values_here(1)
     some(1)
     spread_dv(1)
     sum_heads(1, 0, 2)

time: 89.6 us -> 89.6 us (level)
  no operation moved by 1% of the time
where the time goes in v4:
time: 89.6 us; the launch traced here: 89.4 us
  Pallas kernels  86.8 us (97%)
  local copies, waits for them, and re-layouts  1.92 us (2%)
    pallas_call x1, Pallas kernels, on_device(): pl.pallas_call(kernel, out_shape=(jax.ShapeDtypeStruct((BLK, 512), BF16),...  86.8 us
    unnamed x4, local copies, waits for them, and re-layouts  1.92 us

profile of v4, /device:TPU:1, one launch (start us, length us, event | category | flops | bytes accessed | tf_op | source)
XLA Modules:
  0.0 89.4 jit_solution(15726817802470066845)
XLA Ops:
  0.6 0.0 copy-start
  0.6 0.6 copy-done
  1.3 86.8 %grads.1 = (bf16[128,512]{1,0:T(8,128)(2,1)S(1)}, f32[16,512]{1,0:T(8,128)S(1)}) custom-call(s32[1,5]{1,0:T(1,128)S(1)} %copy-done, bf16[128,4096]{1,0:T(8,128)(2,1)} %bitcast.8, bf16[128,4096]{1,0:T(8,128)(2,1)} %bitcast.9, bf16[128,512]{1,0:T(8,128)(2,1)} %bitcast.10, bf16[128,512]{1,0:T(8,128)(2,1)} %bitcast.11, bf16[128,8192]{1,0:T(8,128)(2,1)} %bitcast.7), custom_call_target="tpu_custom_call" | custom-call | tf_op jit(solution)/shard_map/grads/pallas_call | solution.py:536
  88.1 0.7 copy.10
  88.8 0.6 copy.11
Async XLA Ops:
  0.6 0.7 copy-start
